TPU v7x, 256 devices: a whole 4x4x8 slice. The times are simulated.
256 devices in a mesh: row: 16 (over y, z_lo), col: 16 (over x, z_hi, core).
Axes of the slice: x: 4, y: 4, z: 8 (z_hi: 2, z_lo: 4; z = z_hi * 4 + z_lo), core: 2. Of those that a mesh axis runs over, the one named last changes fastest.
Arguments:
- node_features: bfloat16 [16, 2048, 512], P('col', 'row'), may hold values from -6 to 6
- tile_coords: int32 [16, 16, 2, 128], P('row', 'col'), may hold values from 0 to 15, as said below
- tile_count: int32 [16, 16], P('row', 'col'), may hold values from 32 to 128, as said below
- tile_values: bfloat16 [16, 16, 128, 128, 128], P('row', 'col'), may hold values from -0.25 to 0.25
- weight: bfloat16 [512, 512], replicated, may hold values from -0.25 to 0.25
- cotangent: bfloat16 [16, 2048, 512], P('row', 'col'), may hold values from -6 to 6
Outputs:
- hidden: bfloat16 [16, 2048, 512], P('row', 'col')
- weight_grad: float32 [512, 512], replicated
- feature_grad: bfloat16 [16, 2048, 512], P('col', 'row')
Inputs may be any that keep to these rules, and one draw needn't show every extreme that they name: In each block (i, j), slot k names tile row tile_coords[i, j, 0, k] below 16 and tile column tile_coords[i, j, 1, k] below 16; the 128 pairs of a block are distinct. `tile_count`: the number of used slots of each block; some block uses all 128.
All inputs are finite; a program needn't handle non-finite values.
Results may differ from a plain program's by a relative error of at most 0.028.
Values may be sent and summed in bfloat16 or wider, within the bound.
No kernel may reach another device: no remote copies, remote signals or barrier semaphores. Data moves between devices by JAX's collectives and lax.ppermute only.
A program may use at most 128 MiB of HBM per device.

v0:
```python
import math

import jax
import jax.numpy as jnp
from jax import lax
from jax.sharding import PartitionSpec as P


def silu_slope(pre):
    sigma = jax.nn.sigmoid(pre)
    return sigma * (1.0 + pre * (1.0 - sigma))


def aggregate(values, tile_rows, tile_cols, count, source, out_tiles, transpose):
    slots = values.shape[0]
    tile_size = values.shape[1]
    feature_count = source.shape[2]
    per_block = math.gcd(slots, 32)
    blocks = slots // per_block
    usable = (jnp.arange(slots) < count).astype(jnp.float32)
    entries = (
        values.reshape(blocks, per_block, tile_size, tile_size),
        tile_rows.reshape(blocks, per_block),
        tile_cols.reshape(blocks, per_block),
        usable.reshape(blocks, per_block),
    )

    def advance(total, entry):
        tile_part, row_part, col_part, usable_part = entry
        if transpose:
            pieces = source[row_part]
            product = jnp.einsum(
                "kab,kaf->kbf", tile_part, pieces, preferred_element_type=jnp.float32
            )
            target = col_part
        else:
            pieces = source[col_part]
            product = jnp.einsum(
                "kab,kbf->kaf", tile_part, pieces, preferred_element_type=jnp.float32
            )
            target = row_part
        return (total.at[target].add(product * usable_part[:, None, None]), None)

    start = jnp.zeros((out_tiles, tile_size, feature_count), jnp.float32)
    total, _ = lax.scan(advance, start, entries)
    return total.reshape(out_tiles * tile_size, feature_count)


def body(node_features, tile_coords, tile_count, tile_values, weight, cotangent):
    values = tile_values[0, 0]
    coords = tile_coords[0, 0]
    count = tile_count[0, 0]
    tile_size = values.shape[1]
    feature_count = weight.shape[0]
    group_rows = cotangent.shape[1]
    col_parts = lax.axis_size("col")
    row_parts = lax.axis_size("row")
    nodes_all = group_rows * row_parts * col_parts
    block_rows = group_rows * col_parts
    block_cols = group_rows * row_parts
    row_tiles = block_rows // tile_size
    col_tiles = block_cols // tile_size
    gathered = lax.all_gather(node_features, "row", axis=1, tiled=True)
    source = gathered[0].reshape(col_tiles, tile_size, feature_count)
    partial_rows = aggregate(values, coords[0], coords[1], count, source, row_tiles, False)
    partial_rows = lax.optimization_barrier(partial_rows.astype(jnp.bfloat16)).astype(jnp.float32)
    summed = lax.psum_scatter(
        partial_rows.astype(jnp.bfloat16), "col", scatter_dimension=0, tiled=True
    )
    pre = jnp.dot(summed, weight, preferred_element_type=jnp.float32)
    hidden = jax.nn.silu(pre).astype(jnp.bfloat16)
    grad_pre = (cotangent[0].astype(jnp.float32) * silu_slope(pre)).astype(jnp.bfloat16)
    grad_summed = lax.dot_general(
        grad_pre, weight, (((1,), (1,)), ((), ())), preferred_element_type=jnp.float32
    ).astype(jnp.bfloat16)
    grad_block = lax.all_gather(grad_summed, "col", axis=0, tiled=True)
    term = lax.dot_general(
        summed, grad_pre, (((0,), (0,)), ((), ())), preferred_element_type=jnp.float32
    )
    weight_grad = lax.psum(term, ("row", "col")) / math.sqrt(nodes_all)
    grad_source = grad_block.reshape(row_tiles, tile_size, feature_count)
    back = aggregate(values, coords[0], coords[1], count, grad_source, col_tiles, True)
    back = lax.optimization_barrier(back.astype(jnp.bfloat16)).astype(jnp.float32)
    feature_grad = lax.psum_scatter(
        back.astype(jnp.bfloat16), "row", scatter_dimension=0, tiled=True
    )
    return (hidden[None], weight_grad, feature_grad[None])


def solution(mesh):
    in_specs = (
        P("col", "row", None),
        P("row", "col", None, None),
        P("row", "col"),
        P("row", "col", None, None, None),
        P(),
        P("row", "col", None),
    )
    out_specs = (P("row", "col", None), P(), P("col", "row", None))
    return jax.shard_map(body, mesh=mesh, in_specs=in_specs, out_specs=out_specs, check_vma=False)
```

profile of v0, /device:TPU:6, one launch (start us, length us, event | category | flops | bytes accessed | tf_op | source)
XLA Modules:
  0.0 726.0 jit_solution(8696462391190003510)
XLA Ops:
  7.2 0.0 copy-start
  7.2 0.0 all-gather.3.cloned.1.call-start
  7.2 0.7 all-gather.3.cloned.1.call-update
  7.9 0.0 reduce-scatter.3.cloned.1.call-start
  8.6 0.8 slice_reduce_fusion
  9.4 0.1 reshape_squeeze.17
  9.5 0.1 reshape_squeeze.15
  9.6 90.2 %all-gather.3.cloned.1.call-done = bf16[1,2048,512]{2,1,0:T(8,128)(2,1)} async-done(((bf16[1,128,512]{2,1,0:T(8,128)(2,1)}), bf16[1,2048,512]{2,1,0:T(8,128)(2,1)}) %all-gather.3.cloned.1.call-update) | async-done | bytes 2097168 | tf_op jit(solution)/shard_map/all_gather | solution.py:63
  99.8 0.0 copy-start.2
  99.8 2.5 broadcast.78.clone
  102.2 0.0 copy-done.2
  102.2 112.6 %while.20 = (s32[]{:T(128)}, f32[16,128,512]{2,1,0:T(8,128)}, s32[4,32]{1,0:T(4,128)S(1)}, bf16[4,32,128,128]{3,2,1,0:T(8,128)(2,1)}, s32[4,32]{1,0:T(4,128)S(1)...) while((s32[]{:T(128)}, f32[16,128,512]{2,1,0:T(8,128)}, s32[4,32]{1,0:T(4,128)S(1)}, ...), condition=%wide.region_2.3_spmd, body=%wide.region_0.2_spmd.sunk | while | flops 541066432 | bytes 47191400 | solution.py:45
  102.3 2.7 gather_fusion
  105.0 7.0 broadcast_multiply_fusion.5
  112.0 18.2 %scatter_fusion = f32[16,128,512]{2,1,0:T(8,128)} fusion(f32[16,128,512]{2,1,0:T(8,128)} %get-tuple-element.223, s32[32]{0:T(128)S(1)} %get-tuple-element.203, f32[32,128,512]{2,1,0:T(8,128)} %broadcast_multiply_fusion.5), kind=kCustom, calls=%fused_computation.2.clone.1 | custom fusion | flops 2097152 | bytes 25165952 | tf_op jit(solution)/shard_map/while/body/eval_jaxpr/scatter-add | solution.py:42
  130.2 2.7 gather_fusion
  133.0 7.0 broadcast_multiply_fusion.5
  139.9 18.5 %scatter_fusion = f32[16,128,512]{2,1,0:T(8,128)} fusion(f32[16,128,512]{2,1,0:T(8,128)} %get-tuple-element.223, s32[32]{0:T(128)S(1)} %get-tuple-element.203, f32[32,128,512]{2,1,0:T(8,128)} %broadcast_multiply_fusion.5), kind=kCustom, calls=%fused_computation.2.clone.1 | custom fusion | flops 2097152 | bytes 25165952 | tf_op jit(solution)/shard_map/while/body/eval_jaxpr/scatter-add | solution.py:42
  158.5 2.7 gather_fusion
  161.2 7.0 broadcast_multiply_fusion.5
  168.2 18.5 %scatter_fusion = f32[16,128,512]{2,1,0:T(8,128)} fusion(f32[16,128,512]{2,1,0:T(8,128)} %get-tuple-element.223, s32[32]{0:T(128)S(1)} %get-tuple-element.203, f32[32,128,512]{2,1,0:T(8,128)} %broadcast_multiply_fusion.5), kind=kCustom, calls=%fused_computation.2.clone.1 | custom fusion | flops 2097152 | bytes 25165952 | tf_op jit(solution)/shard_map/while/body/eval_jaxpr/scatter-add | solution.py:42
  186.7 2.7 gather_fusion
  189.5 7.0 broadcast_multiply_fusion.5
  196.5 18.4 %scatter_fusion = f32[16,128,512]{2,1,0:T(8,128)} fusion(f32[16,128,512]{2,1,0:T(8,128)} %get-tuple-element.223, s32[32]{0:T(128)S(1)} %get-tuple-element.203, f32[32,128,512]{2,1,0:T(8,128)} %broadcast_multiply_fusion.5), kind=kCustom, calls=%fused_computation.2.clone.1 | custom fusion | flops 2097152 | bytes 25165952 | tf_op jit(solution)/shard_map/while/body/eval_jaxpr/scatter-add | solution.py:42
  214.8 0.0 copy-start.4
  214.8 3.8 convert_element_type.37
  218.7 0.0 reduce-scatter.3.cloned.1.call-update
  218.7 0.0 all-gather.5.cloned.1.call-start
  218.7 86.5 %reduce-scatter.3.cloned.1.call-done = bf16[128,512]{1,0:T(8,128)(2,1)} async-done(((bf16[2048,512]{1,0:T(8,128)(2,1)}), bf16[128,512]{1,0:T(8,128)(2,1)}) %reduce-scatter.3.cloned.1.call-update) | async-done | bytes 131088 | tf_op jit(solution)/shard_map/reduce_scatter | solution.py:67
  305.3 0.0 copy-done
  305.3 1.1 fusion.22
  306.4 0.0 copy-done.4
  306.4 1.0 convolution_convert_fusion
  307.4 0.0 all-gather.5.cloned.1.call-update
  307.4 0.0 copy-start.3
  307.4 0.0 all-reduce.2.cloned.1.call-start
  307.5 6.4 copy.9
  313.8 0.0 copy-done.3
  313.8 1.3 fusion.20
  315.2 0.0 all-reduce.2.cloned.1.call-update
  315.2 0.0 reduce-scatter.5.cloned.1.call-start
  315.3 52.3 %all-gather.5.cloned.1.call-done = bf16[2048,512]{1,0:T(8,128)(2,1)} async-done(((bf16[128,512]{1,0:T(8,128)(2,1)}), bf16[2048,512]{1,0:T(8,128)(2,1)}) %all-gather.5.cloned.1.call-update) | async-done | bytes 2097168 | tf_op jit(solution)/shard_map/all_gather | solution.py:76
  367.5 0.0 copy-start.1
  367.5 2.5 broadcast.78
  370.0 0.0 copy-done.1
  370.0 112.6 %while.21 = (s32[]{:T(128)}, f32[16,128,512]{2,1,0:T(8,128)}, s32[4,32]{1,0:T(4,128)S(1)}, bf16[4,32,128,128]{2,3,1,0:T(8,128)(2,1)}, s32[4,32]{1,0:T(4,128)S(1)...) while((s32[]{:T(128)}, f32[16,128,512]{2,1,0:T(8,128)}, s32[4,32]{1,0:T(4,128)S(1)}, ...), condition=%wide.region_7.8_spmd, body=%wide.region_5.7_spmd.sunk | while | flops 541066432 | bytes 47191400 | solution.py:45
  370.0 2.8 gather_fusion.1
  372.8 7.0 broadcast_multiply_fusion.6
  379.7 18.5 %scatter_fusion.1 = f32[16,128,512]{2,1,0:T(8,128)} fusion(f32[16,128,512]{2,1,0:T(8,128)} %get-tuple-element.247, s32[32]{0:T(128)S(1)} %get-tuple-element.212, f32[32,128,512]{2,1,0:T(8,128)} %broadcast_multiply_fusion.6), kind=kCustom, calls=%fused_computation.3.clone.1 | custom fusion | flops 2097152 | bytes 25165952 | tf_op jit(solution)/shard_map/while/body/eval_jaxpr/scatter-add | solution.py:42
  398.2 2.8 gather_fusion.1
  401.0 7.0 broadcast_multiply_fusion.6
  408.0 18.2 %scatter_fusion.1 = f32[16,128,512]{2,1,0:T(8,128)} fusion(f32[16,128,512]{2,1,0:T(8,128)} %get-tuple-element.247, s32[32]{0:T(128)S(1)} %get-tuple-element.212, f32[32,128,512]{2,1,0:T(8,128)} %broadcast_multiply_fusion.6), kind=kCustom, calls=%fused_computation.3.clone.1 | custom fusion | flops 2097152 | bytes 25165952 | tf_op jit(solution)/shard_map/while/body/eval_jaxpr/scatter-add | solution.py:42
  426.2 2.8 gather_fusion.1
  429.0 7.0 broadcast_multiply_fusion.6
  435.9 18.4 %scatter_fusion.1 = f32[16,128,512]{2,1,0:T(8,128)} fusion(f32[16,128,512]{2,1,0:T(8,128)} %get-tuple-element.247, s32[32]{0:T(128)S(1)} %get-tuple-element.212, f32[32,128,512]{2,1,0:T(8,128)} %broadcast_multiply_fusion.6), kind=kCustom, calls=%fused_computation.3.clone.1 | custom fusion | flops 2097152 | bytes 25165952 | tf_op jit(solution)/shard_map/while/body/eval_jaxpr/scatter-add | solution.py:42
  454.4 2.8 gather_fusion.1
  457.2 7.0 broadcast_multiply_fusion.6
  464.1 18.4 %scatter_fusion.1 = f32[16,128,512]{2,1,0:T(8,128)} fusion(f32[16,128,512]{2,1,0:T(8,128)} %get-tuple-element.247, s32[32]{0:T(128)S(1)} %get-tuple-element.212, f32[32,128,512]{2,1,0:T(8,128)} %broadcast_multiply_fusion.6), kind=kCustom, calls=%fused_computation.3.clone.1 | custom fusion | flops 2097152 | bytes 25165952 | tf_op jit(solution)/shard_map/while/body/eval_jaxpr/scatter-add | solution.py:42
  482.6 3.8 convert_element_type.44
  486.4 0.0 reduce-scatter.5.cloned.1.call-update
  486.4 0.7 fusion.17
  487.1 138.2 %all-reduce.2.cloned.1.call-done = f32[512,512]{1,0:T(8,128)} async-done(((f32[512,512]{1,0:T(8,128)}), f32[512,512]{1,0:T(8,128)}) %all-reduce.2.cloned.1.call-update) | async-done | bytes 1048592 | tf_op jit(solution)/shard_map/psum | solution.py:80
  625.3 2.3 broadcast_multiply_fusion.2
  627.6 91.9 %reduce-scatter.5.cloned.1.call-done = bf16[128,512]{1,0:T(8,128)(2,1)} async-done(((bf16[2048,512]{1,0:T(8,128)(2,1)}), bf16[128,512]{1,0:T(8,128)(2,1)}) %reduce-scatter.5.cloned.1.call-update) | async-done | bytes 131088 | tf_op jit(solution)/shard_map/reduce_scatter | solution.py:84
  (25 shorter events, 0.2 us)
Async XLA Ops:
  7.2 298.1 %copy-start = (bf16[512,512]{1,0:T(8,128)(2,1)S(1)}, bf16[512,512]{1,0:T(8,128)(2,1)}, u32[]{:S(2)}) copy-start(bf16[512,512]{1,0:T(8,128)(2,1)} %param.14) | copy-start | bytes 1572868
  7.2 92.6 %all-gather.3.cloned.1.call-start = ((), (), s32[]{:S(2)}) async-start(), calls=%async_computation.2 | async-start | bytes 2228224 | tf_op jit(solution)/shard_map/all_gather | solution.py:63
  7.9 297.4 %reduce-scatter.3.cloned.1.call-start = ((), (), s32[]{:S(2)}) async-start(), calls=%async_computation.3 | async-start | bytes 2228224 | tf_op jit(solution)/shard_map/reduce_scatter | solution.py:67
  99.8 2.5 copy-start.2
  214.8 91.6 %copy-start.4 = (bf16[1,128,512]{2,1,0:T(8,128)(2,1)S(1)}, bf16[1,128,512]{2,1,0:T(8,128)(2,1)}, u32[]{:S(2)}) copy-start(bf16[1,128,512]{2,1,0:T(8,128)(2,1)} %param.15) | copy-start | bytes 393220
  218.7 148.8 %all-gather.5.cloned.1.call-start = ((), (), s32[]{:S(2)}) async-start(), calls=%async_computation.5 | async-start | bytes 2228224 | tf_op jit(solution)/shard_map/all_gather | solution.py:76
  307.4 6.4 copy-start.3
  307.4 317.9 %all-reduce.2.cloned.1.call-start = ((), (), s32[]{:S(2)}) async-start(), calls=%async_computation.4 | async-start | bytes 2097152 | tf_op jit(solution)/shard_map/psum | solution.py:80
  315.2 404.3 %reduce-scatter.5.cloned.1.call-start = ((), (), s32[]{:S(2)}) async-start(), calls=%async_computation.6 | async-start | bytes 2228224 | tf_op jit(solution)/shard_map/reduce_scatter | solution.py:84
  367.5 2.5 copy-start.1
Sparse Core Ops, SparseCore 0:
  9.8 89.9 all-gather.2
  218.8 86.4 reduce-scatter.2
  308.5 58.9 all-gather.4
  373.4 251.8 all-reduce.1
  628.4 91.0 reduce-scatter.4
where the time goes:
time: 727 us; the launch traced here: 726 us
  waiting for transfers between devices  460 us (63%)
  other arithmetic  158 us (22%)
  matrix products  59.2 us (8%)
  local copies, waits for them, and re-layouts  34.3 us (5%)
  between operations  14.5 us (2%)
    scatter-add x8, other arithmetic, advance(): return (total.at[target].add(product * usable_part[:, None, None]), None)  147 us
    psum x1, waiting for transfers between devices, body(): weight_grad = lax.psum(term, ('row', 'col')) / math.sqrt(nodes_all)  138 us
    reduce_scatter x1, waiting for transfers between devices, body(): lax.psum_scatter(back.astype(jnp.bfloat16), 'row', scatter_dimension=0, t...  91.9 us
    all_gather x1, waiting for transfers between devices, body(): gathered = lax.all_gather(node_features, 'row', axis=1, tiled=True)  90.2 us
    reduce_scatter x1, waiting for transfers between devices, body(): lax.psum_scatter(partial_rows.astype(jnp.bfloat16), 'col', scatter_dimens...  86.5 us
    all_gather x1, waiting for transfers between devices, body(): grad_block = lax.all_gather(grad_summed, 'col', axis=0, tiled=True)  52.3 us
    dot_general x4, matrix products, advance(): jnp.einsum('kab,kaf->kbf', tile_part, pieces, preferred_element_type=jnp....  27.9 us
    dot_general x4, matrix products, advance(): jnp.einsum('kab,kbf->kaf', tile_part, pieces, preferred_element_type=jnp....  27.9 us
  transfers between devices with their start and end apart: 5, of which 5 were waited for; matrix products, arithmetic and copies ran while one was open for 18% of the time, Pallas kernels for 0%

commit v1 on v0

v1 whole, which is shorter than its diff:
```python
import math

import jax
import jax.numpy as jnp
from jax import lax
from jax.experimental import pallas as pl
from jax.experimental.pallas import tpu as pltpu
from jax.sharding import PartitionSpec as P

Y = 4
Z = 4
X = 4
H = 2
C = 2
TILE = 128


def row_shift(data, axis, step):
    pairs = []
    for r in range(Y * Z):
        y, z = divmod(r, Z)
        if axis == "y":
            source = (y + step) % Y * Z + z
        else:
            source = y * Z + (z + step) % Z
        pairs.append((source, r))
    return lax.ppermute(data, "row", pairs)


def col_shift(data, axis, step):
    pairs = []
    for c in range(X * H * C):
        x, h, k = c // (H * C), c // C % H, c % C
        if axis == "x":
            x = (x + step) % X
        elif axis == "h":
            h = (h + step) % H
        else:
            k = (k + step) % C
        pairs.append(((x * H + h) * C + k, c))
    return lax.ppermute(data, "col", pairs)


def densify_kernel(place_ref, count_ref, values_ref, forward_ref, backward_ref):
    size = forward_ref.shape[0]
    zeros = jnp.zeros((TILE, size), forward_ref.dtype)

    def clear(i, _):
        rows = pl.ds(pl.multiple_of(i * TILE, TILE), TILE)
        forward_ref[rows, :] = zeros
        backward_ref[rows, :] = zeros
        return 0

    lax.fori_loop(0, size // TILE, clear, 0)

    def put(k, _):
        r = pl.ds(pl.multiple_of(place_ref[0, k] * TILE, TILE), TILE)
        c = pl.ds(pl.multiple_of(place_ref[1, k] * TILE, TILE), TILE)
        tile = values_ref[k]
        forward_ref[r, c] = tile
        backward_ref[c, r] = tile.T
        return 0

    lax.fori_loop(0, count_ref[0], put, 0)


def densify(values, place, count):
    size = 16 * TILE
    dense = jax.ShapeDtypeStruct((size, size), values.dtype)
    return pl.pallas_call(
        densify_kernel,
        out_shape=(dense, dense),
        in_specs=[
            pl.BlockSpec(memory_space=pltpu.SMEM),
            pl.BlockSpec(memory_space=pltpu.SMEM),
            pl.BlockSpec(memory_space=pltpu.VMEM),
        ],
        out_specs=(
            pl.BlockSpec(memory_space=pltpu.VMEM),
            pl.BlockSpec(memory_space=pltpu.VMEM),
        ),
        compiler_params=pltpu.CompilerParams(vmem_limit_bytes=40 * 1024 * 1024),
        cost_estimate=pl.CostEstimate(
            flops=0, bytes_accessed=20 * 1024 * 1024, transcendentals=0
        ),
    )(place, count, values)


def f32(value):
    return value.astype(jnp.float32)


def bf16(value):
    return value.astype(jnp.bfloat16)


def matmul(a, b):
    return jnp.dot(a, b, preferred_element_type=jnp.float32)


def body(node_features, tile_coords, tile_count, tile_values, weight, cotangent):
    features = node_features[0]
    me_row = lax.axis_index("row")
    me_col = lax.axis_index("col")
    my, mz = me_row // Z, me_row % Z
    mx, mh, mk = me_col // (H * C), me_col // C % H, me_col % C
    nodes_all = TILE * Y * Z * X * H * C

    tr, tc = tile_coords[0, 0, 0], tile_coords[0, 0, 1]
    place_r = ((tr + mk) % C) * (X * H) + ((tr // (H * C) - mx) % X) * H + (tr // C + mh) % H
    place_c = ((tc // Z - my) % Y) * Z + (tc - mz) % Z
    forward, backward = densify(
        tile_values[0, 0], jnp.stack([place_r, place_c]), tile_count[0]
    )

    run = jnp.concatenate([features] + [row_shift(features, "z", s) for s in (1, 2, 3)])
    source = jnp.concatenate([run] + [row_shift(run, "y", s) for s in (1, 2, 3)])

    half = 8 * TILE
    away = bf16(matmul(forward[half:], source))
    home = matmul(forward[:half], source)
    home = bf16(home + f32(col_shift(away, "k", 1)))
    quarter = 2 * TILE
    total = f32(home[:quarter])
    for s in (1, 2, 3):
        total += f32(col_shift(home[s * quarter : (s + 1) * quarter], "x", X - s))
    summed = bf16(total[:TILE] + f32(col_shift(bf16(total[TILE:]), "h", 1)))

    pre = matmul(summed, weight)
    sigma = jax.nn.sigmoid(pre)
    hidden = bf16(pre * sigma)
    grad_pre = bf16(f32(cotangent[0]) * (sigma * (1.0 + pre * (1.0 - sigma))))
    grad_summed = bf16(
        lax.dot_general(
            grad_pre, weight, (((1,), (1,)), ((), ())), preferred_element_type=jnp.float32
        )
    )
    term = lax.dot_general(
        summed, grad_pre, (((0,), (0,)), ((), ())), preferred_element_type=jnp.float32
    )

    pair = jnp.concatenate([grad_summed, col_shift(grad_summed, "h", 1)])
    eight = jnp.concatenate([pair] + [col_shift(pair, "x", s) for s in (1, 2, 3)])
    grads = jnp.concatenate([eight, col_shift(eight, "k", 1)])

    def cut(value, index, size):
        return lax.dynamic_slice_in_dim(value, index * size, size, 0)

    part = cut(term, mk, 256) + f32(col_shift(bf16(cut(term, 1 - mk, 256)), "k", 1))
    piece = cut(part, mx, 64)
    for s in (1, 2, 3):
        piece += f32(col_shift(bf16(cut(part, (mx + s) % X, 64)), "x", X - s))
    piece = cut(piece, mh, 32) + f32(col_shift(bf16(cut(piece, 1 - mh, 32)), "h", 1))
    for axis, me in (("y", my), ("z", mz)):
        sent = bf16(piece)
        parts = [sent] + [row_shift(sent, axis, s) for s in (1, 2, 3)]
        ordered = lax.dynamic_slice_in_dim(jnp.stack(parts + parts[:3]), (4 - me) % 4, 4, 0)
        piece = f32(ordered[0]) + f32(ordered[1]) + f32(ordered[2]) + f32(ordered[3])
    sent = bf16(piece / math.sqrt(nodes_all))
    other = col_shift(sent, "h", 1)
    sent = jnp.where(mh == 0, jnp.concatenate([sent, other]), jnp.concatenate([other, sent]))
    parts = [sent] + [col_shift(sent, "x", s) for s in (1, 2, 3)]
    sent = lax.dynamic_slice_in_dim(
        jnp.concatenate(parts + parts[:3]), ((X - mx) % X) * 64, 256, 0
    )
    other = col_shift(sent, "k", 1)
    weight_grad = f32(
        jnp.where(mk == 0, jnp.concatenate([sent, other]), jnp.concatenate([other, sent]))
    )

    block = Z * TILE
    got = []
    for s in (2, 1, 3):
        back = bf16(matmul(backward[s * block : (s + 1) * block], grads))
        got.append(row_shift(back, "y", Y - s))
    total = matmul(backward[:block], grads)
    for arrived in got:
        total += f32(arrived)
    result = total[:TILE]
    for s in (1, 2, 3):
        result += f32(row_shift(bf16(total[s * TILE : (s + 1) * TILE]), "z", Z - s))
    return (hidden[None], weight_grad, bf16(result)[None])


def solution(mesh):
    in_specs = (
        P("col", "row", None),
        P("row", "col", None, None),
        P("row", "col"),
        P("row", "col", None, None, None),
        P(),
        P("row", "col", None),
    )
    out_specs = (P("row", "col", None), P(), P("col", "row", None))
    return jax.shard_map(body, mesh=mesh, in_specs=in_specs, out_specs=out_specs, check_vma=False)
```

time: 727 us -> 188 us (0.26)
  waiting for transfers between devices: 460 us -> 80.5 us
  other arithmetic: 158 us -> 4.7 us
  starting transfers between devices: 0.2 us -> 66.4 us
  matrix products: 59.2 us -> 15.8 us
  local copies, waits for them, and re-layouts: 34.3 us -> 4.76 us
  between operations: 14.5 us -> 1.95 us
  Pallas kernels: 0 us -> 12.3 us
    reduce_scatter x2 -> x0, waiting for transfers between devices: 178 us -> none  [the longest x1 91.9 us: body(): lax.psum_scatter(back.astype(jnp.bfloat16), 'row', scatter_dimension=0, t...]
    scatter-add x8 -> x0, other arithmetic: 147 us -> none  [advance(): return (total.at[target].add(product * usable_part[:, None, None]), None)]
    all_gather x2 -> x0, waiting for transfers between devices: 142 us -> none  [the longest x1 90.2 us: body(): gathered = lax.all_gather(node_features, 'row', axis=1, tiled=True)]
    psum x1 -> x0, waiting for transfers between devices: 138 us -> none  [body(): weight_grad = lax.psum(term, ('row', 'col')) / math.sqrt(nodes_all)]
    ppermute x0 -> x38, waiting for transfers between devices: none -> 80.5 us  [the longest x18 55.4 us: row_shift(): return lax.ppermute(data, 'row', pairs)]
    ppermute x0 -> x38, starting transfers between devices: none -> 66.4 us  [the longest x20 45.1 us: col_shift(): return lax.ppermute(data, 'col', pairs)]
    dot_general x9 -> x7, matrix products: 56.9 us -> 15.1 us  [matmul(): return jnp.dot(a, b, preferred_element_type=jnp.float32)]
    gather x8 -> x0, local copies, waits for them, and re-layouts: 22 us -> none  [the longest x4 11 us: advance(): pieces = source[row_part]]
  transfers between devices with their start and end apart: 5 -> 38, of which waited for: 5 -> 22; matrix products, arithmetic and copies ran while one was open for 18% -> 8% of each run, Pallas kernels for 0% -> 7%
where the time goes in v1:
time: 188 us; the launch traced here: 186 us
  waiting for transfers between devices  80.5 us (43%)
  starting transfers between devices  66.4 us (35%)
  matrix products  15.8 us (8%)
  Pallas kernels  12.3 us (7%)
  local copies, waits for them, and re-layouts  4.76 us (3%)
  other arithmetic  4.7 us (2%)
  between operations  1.95 us (1%)
    ppermute x18, waiting for transfers between devices, row_shift(): return lax.ppermute(data, 'row', pairs)  55.4 us
    ppermute x20, starting transfers between devices, col_shift(): return lax.ppermute(data, 'col', pairs)  45.1 us
    ppermute x20, waiting for transfers between devices, col_shift(): return lax.ppermute(data, 'col', pairs)  25.1 us
    ppermute x18, starting transfers between devices, row_shift(): return lax.ppermute(data, 'row', pairs)  21.3 us
    dot_general x7, matrix products, matmul(): return jnp.dot(a, b, preferred_element_type=jnp.float32)  15.1 us
    pallas_call x1, Pallas kernels, densify(): pl.pallas_call(densify_kernel, out_shape=(dense, dense), in_specs=[pl.Blo...  12.3 us
  transfers between devices with their start and end apart: 38, of which 22 were waited for; matrix products, arithmetic and copies ran while one was open for 8% of the time, Pallas kernels for 7%

profile of v1, /device:TPU:6, one launch (start us, length us, event | category | flops | bytes accessed | tf_op | source)
XLA Modules:
  0.0 186.4 jit_solution(6531336506973406865)
XLA Ops:
  0.6 4.7 %collective-permute-start = (bf16[128,512]{1,0:T(8,128)(2,1)}, bf16[128,512]{1,0:T(8,128)(2,1)S(1)}, u32[]{:S(2)}, u32[]{:S(2)}) collective-permute-start(bf16[128,512]{1,0:T(8,128)(2,1)} %bitcast.78), channel_id=1, source_target_pairs={{16,0},{32,16},{48,32},{0,48},{80,64},{96,80},{112,96},{64,112},{1... | collective-permute-start | bytes 393224 | tf_op jit(solution)/shard_map/ppermute | solution.py:27
  5.3 0.7 collective-permute-start.2
  6.0 0.9 constant_dynamic-update-slice_fusion.6
  7.0 2.6 %collective-permute-done = bf16[128,512]{1,0:T(8,128)(2,1)S(1)} collective-permute-done((bf16[128,512]{1,0:T(8,128)(2,1)}, bf16[128,512]{1,0:T(8,128)(2,1)S(1)}, u32[]{:S(2)}, u32[]{:S(2)}) %collective-permute-start) | collective-permute-done | bytes 131104 | tf_op jit(solution)/shard_map/ppermute | solution.py:27
  9.6 7.2 %collective-permute-done.1 = bf16[128,512]{1,0:T(8,128)(2,1)S(1)} collective-permute-done((bf16[128,512]{1,0:T(8,128)(2,1)}, bf16[128,512]{1,0:T(8,128)(2,1)S(1)}, u32[]{:S(2)}, u32[]{:S(2)}) %collective-permute-start.1) | collective-permute-done | bytes 131104 | tf_op jit(solution)/shard_map/ppermute | solution.py:27
  16.8 0.9 pad_maximum_fusion
  17.7 3.1 %collective-permute-start.3 = (bf16[512,512]{1,0:T(8,128)(2,1)S(1)}, bf16[512,512]{1,0:T(8,128)(2,1)S(1)}, u32[]{:S(2)}, u32[]{:S(2)}) collective-permute-start(bf16[512,512]{1,0:T(8,128)(2,1)S(1)} %pad_maximum_fusion), channel_id=1, source_target_pairs={{64,0},{80,16},{96,32},{112,48},{128,64},{144,80},{160,96},{176,11... | collective-permute-start | bytes 1572872 | tf_op jit(solution)/shard_map/ppermute | solution.py:27
  20.8 0.8 fusion.44
  21.6 0.7 collective-permute-start.4
  23.0 2.2 %copy-done.1 = bf16[1,1,128,128,128]{4,3,2,1,0:T(8,128)(2,1)S(1)} copy-done((bf16[1,1,128,128,128]{4,3,2,1,0:T(8,128)(2,1)S(1)}, bf16[1,1,128,128,128]{4,3,2,1,0:T(8,128)(2,1)}, u32[]{:S(2)}) %copy-start.1) | copy-done | bytes 4194328
  25.2 12.3 %shard_map.85 = (bf16[2048,2048]{1,0:T(8,128)(2,1)S(1)}, bf16[2048,2048]{1,0:T(8,128)(2,1)}) custom-call(s32[2,128]{1,0:T(2,128)S(1)} %pad_add_fusion.place_ref, s32[1]{0:T(128)} %bitcast.76.count_ref, bf16[128,128,128]{2,1,0:T(8,128)(2,1)S(1)} %bitcast.77), custom_call_target="tpu_custom_call" | custom-call | bytes 20971520 | tf_op jit(solution)/shard_map/pallas_call | solution.py:70
  37.5 5.3 %collective-permute-done.3 = bf16[512,512]{1,0:T(8,128)(2,1)S(1)} collective-permute-done((bf16[512,512]{1,0:T(8,128)(2,1)S(1)}, bf16[512,512]{1,0:T(8,128)(2,1)S(1)}, u32[]{:S(2)}, u32[]{:S(2)}) %collective-permute-start.3) | collective-permute-done | bytes 524320 | tf_op jit(solution)/shard_map/ppermute | solution.py:27
  42.9 5.6 %collective-permute-done.5 = bf16[512,512]{1,0:T(8,128)(2,1)S(1)} collective-permute-done((bf16[512,512]{1,0:T(8,128)(2,1)S(1)}, bf16[512,512]{1,0:T(8,128)(2,1)S(1)}, u32[]{:S(2)}, u32[]{:S(2)}) %collective-permute-start.5) | collective-permute-done | bytes 524320 | tf_op jit(solution)/shard_map/ppermute | solution.py:27
  48.4 2.3 %fusion.14 = bf16[1024,512]{1,0:T(8,128)(2,1)S(1)} fusion(bf16[2048,512]{1,0:T(8,128)(2,1)S(1)} %constant_dynamic-update-slice_fusion, bf16[2048,2048]{1,0:T(8,128)(2,1)S(1)} %get-tuple-element.5), kind=kOutput, calls=%fused_computation.13 | convolution fusion | flops 2148007936 | bytes 7340032 | tf_op jit(solution)/shard_map/dot_general | solution.py:98
  50.9 2.6 %collective-permute-done.6 = bf16[1024,512]{1,0:T(8,128)(2,1)S(1)} collective-permute-done((bf16[1024,512]{1,0:T(8,128)(2,1)S(1)}, bf16[1024,512]{1,0:T(8,128)(2,1)S(1)}, u32[]{:S(2)}, u32[]{:S(2)}) %collective-permute-start.6) | collective-permute-done | bytes 1048608 | tf_op jit(solution)/shard_map/ppermute | solution.py:41
  53.5 2.3 %add_convert_fusion = bf16[1024,512]{1,0:T(8,128)(2,1)S(1)} fusion(bf16[1024,512]{1,0:T(8,128)(2,1)S(1)} %collective-permute-done.6, bf16[2048,512]{1,0:T(8,128)(2,1)S(1)} %constant_dynamic-update-slice_fusion, bf16[2048,2048]{1,0:T(8,128)(2,1)S(1)} %get-tuple-element.5), kind=kOutput, calls=%fused_computation.12 | convolution fusion | flops 2149056512 | bytes 8388608 | tf_op jit(solution)/shard_map/dot_general | solution.py:98
  55.9 3.6 %collective-permute-start.9 = (bf16[256,512]{1,0:T(8,128)(2,1)S(1)}, bf16[256,512]{1,0:T(8,128)(2,1)S(1)}, u32[]{:S(2)}, u32[]{:S(2)}) collective-permute-start(bf16[256,512]{1,0:T(8,128)(2,1)S(1)} %get-tuple-element.14), channel_id=1, source_target_pairs={{4,0},{5,1},{6,2},{7,3},{8,4},{9,5},{10,6},{11,7},{12,8},{13,9},{1... | collective-permute-start | bytes 786440 | tf_op jit(solution)/shard_map/ppermute | solution.py:41
  59.6 1.3 collective-permute-start.8
  60.8 2.1 %collective-permute-start.7 = (bf16[256,512]{1,0:T(8,128)(2,1)S(1)}, bf16[256,512]{1,0:T(8,128)(2,1)S(1)}, u32[]{:S(2)}, u32[]{:S(2)}) collective-permute-start(bf16[256,512]{1,0:T(8,128)(2,1)S(1)} %get-tuple-element.13), channel_id=1, source_target_pairs={{12,0},{13,1},{14,2},{15,3},{0,4},{1,5},{2,6},{3,7},{4,8},{5,9},{6... | collective-permute-start | bytes 786440 | tf_op jit(solution)/shard_map/ppermute | solution.py:41
  63.0 3.3 %collective-permute-done.9 = bf16[256,512]{1,0:T(8,128)(2,1)S(1)} collective-permute-done((bf16[256,512]{1,0:T(8,128)(2,1)S(1)}, bf16[256,512]{1,0:T(8,128)(2,1)S(1)}, u32[]{:S(2)}, u32[]{:S(2)}) %collective-permute-start.9) | collective-permute-done | bytes 262176 | tf_op jit(solution)/shard_map/ppermute | solution.py:41
  66.2 6.5 %collective-permute-done.8 = bf16[256,512]{1,0:T(8,128)(2,1)S(1)} collective-permute-done((bf16[256,512]{1,0:T(8,128)(2,1)S(1)}, bf16[256,512]{1,0:T(8,128)(2,1)S(1)}, u32[]{:S(2)}, u32[]{:S(2)}) %collective-permute-start.8) | collective-permute-done | bytes 262176 | tf_op jit(solution)/shard_map/ppermute | solution.py:41
  72.9 8.1 %collective-permute-start.10 = (bf16[128,512]{1,0:T(8,128)(2,1)S(1)}, bf16[128,512]{1,0:T(8,128)(2,1)S(1)}, u32[]{:S(2)}, u32[]{:S(2)}) collective-permute-start(bf16[128,512]{1,0:T(8,128)(2,1)S(1)} %slice.164), channel_id=1, source_target_pairs={{2,0},{3,1},{0,2},{1,3},{6,4},{7,5},{4,6},{5,7},{10,8},{11,9},{8,1... | collective-permute-start | bytes 393224 | tf_op jit(solution)/shard_map/ppermute | solution.py:41
  81.1 5.3 %collective-permute-done.10 = bf16[128,512]{1,0:T(8,128)(2,1)S(1)} collective-permute-done((bf16[128,512]{1,0:T(8,128)(2,1)S(1)}, bf16[128,512]{1,0:T(8,128)(2,1)S(1)}, u32[]{:S(2)}, u32[]{:S(2)}) %collective-permute-start.10) | collective-permute-done | bytes 131104 | tf_op jit(solution)/shard_map/ppermute | solution.py:41
  86.4 0.2 fusion.57
  86.6 0.4 fusion.55
  87.1 0.3 collective-permute-start.11
  87.5 1.4 collective-permute-done.11
  89.1 4.8 %collective-permute-start.13 = (bf16[64,512]{1,0:T(8,128)(2,1)S(1)}, bf16[64,512]{1,0:T(8,128)(2,1)S(1)}, u32[]{:S(2)}, u32[]{:S(2)}) collective-permute-start(bf16[64,512]{1,0:T(8,128)(2,1)S(1)} %get-tuple-element.21), channel_id=1, source_target_pairs={{8,0},{9,1},{10,2},{11,3},{12,4},{13,5},{14,6},{15,7},{0,8},{1,9},... | collective-permute-start | bytes 196616 | tf_op jit(solution)/shard_map/ppermute | solution.py:41
  93.9 0.3 constant_dynamic-update-slice_fusion.32
  94.2 5.4 %collective-permute-start.27 = (bf16[128,512]{1,0:T(8,128)(2,1)S(1)}, bf16[128,512]{1,0:T(8,128)(2,1)S(1)}, u32[]{:S(2)}, u32[]{:S(2)}) collective-permute-start(bf16[128,512]{1,0:T(8,128)(2,1)S(1)} %get-tuple-element.34), channel_id=1, source_target_pairs={{2,0},{3,1},{0,2},{1,3},{6,4},{7,5},{4,6},{5,7},{10,8},{11,9},{8,1... | collective-permute-start | bytes 393224 | tf_op jit(solution)/shard_map/ppermute | solution.py:41
  99.6 3.9 %collective-permute-start.15 = (bf16[32,512]{1,0:T(8,128)(2,1)S(1)}, bf16[32,512]{1,0:T(8,128)(2,1)S(1)}, u32[]{:S(2)}, u32[]{:S(2)}) collective-permute-start(bf16[32,512]{1,0:T(8,128)(2,1)S(1)} %dynamic-slice_convert_fusion.4), channel_id=1, source_target_pairs={{2,0},{3,1},{0,2},{1,3},{6,4},{7,5},{4,6},{5,7},{10,8},{11,9},{8,1... | collective-permute-start | bytes 98312 | tf_op jit(solution)/shard_map/ppermute | solution.py:41
  103.6 1.2 collective-permute-done.27
  104.7 3.4 %collective-permute-start.28 = (bf16[256,512]{1,0:T(8,128)(2,1)S(1)}, bf16[256,512]{1,0:T(8,128)(2,1)S(1)}, u32[]{:S(2)}, u32[]{:S(2)}) collective-permute-start(bf16[256,512]{1,0:T(8,128)(2,1)S(1)} %pad_maximum_fusion.1), channel_id=1, source_target_pairs={{4,0},{5,1},{6,2},{7,3},{8,4},{9,5},{10,6},{11,7},{12,8},{13,9},{1... | collective-permute-start | bytes 786440 | tf_op jit(solution)/shard_map/ppermute | solution.py:41
  108.2 2.8 %collective-permute-start.30 = (bf16[256,512]{1,0:T(8,128)(2,1)S(1)}, bf16[256,512]{1,0:T(8,128)(2,1)S(1)}, u32[]{:S(2)}, u32[]{:S(2)}) collective-permute-start(bf16[256,512]{1,0:T(8,128)(2,1)S(1)} %pad_maximum_fusion.1), channel_id=1, source_target_pairs={{12,0},{13,1},{14,2},{15,3},{0,4},{1,5},{2,6},{3,7},{4,8},{5,9},{6... | collective-permute-start | bytes 786440 | tf_op jit(solution)/shard_map/ppermute | solution.py:41
  111.1 2.1 %collective-permute-start.17 = (bf16[32,512]{1,0:T(8,128)(2,1)S(1)}, bf16[32,512]{1,0:T(8,128)(2,1)S(1)}, u32[]{:S(2)}, u32[]{:S(2)}) collective-permute-start(bf16[32,512]{1,0:T(8,128)(2,1)S(1)} %get-tuple-element.12), channel_id=1, source_target_pairs={{128,0},{144,16},{160,32},{176,48},{192,64},{208,80},{224,96},{240... | collective-permute-start | bytes 98312 | tf_op jit(solution)/shard_map/ppermute | solution.py:27
  113.2 1.8 collective-permute-done.16
  114.9 1.6 collective-permute-done.17
  116.6 3.5 %collective-permute-done.18 = bf16[32,512]{1,0:T(8,128)(2,1)S(1)} collective-permute-done((bf16[32,512]{1,0:T(8,128)(2,1)S(1)}, bf16[32,512]{1,0:T(8,128)(2,1)S(1)}, u32[]{:S(2)}, u32[]{:S(2)}) %collective-permute-start.18) | collective-permute-done | bytes 32800 | tf_op jit(solution)/shard_map/ppermute | solution.py:27
  120.2 2.3 %collective-permute-start.20 = (bf16[32,512]{1,0:T(8,128)(2,1)S(1)}, bf16[32,512]{1,0:T(8,128)(2,1)S(1)}, u32[]{:S(2)}, u32[]{:S(2)}) collective-permute-start(bf16[32,512]{1,0:T(8,128)(2,1)S(1)} %bitcast.83), channel_id=1, source_target_pairs={{32,0},{48,16},{0,32},{16,48},{96,64},{112,80},{64,96},{80,112},{1... | collective-permute-start | bytes 98312 | tf_op jit(solution)/shard_map/ppermute | solution.py:27
  122.5 1.9 %collective-permute-start.21 = (bf16[32,512]{1,0:T(8,128)(2,1)S(1)}, bf16[32,512]{1,0:T(8,128)(2,1)S(1)}, u32[]{:S(2)}, u32[]{:S(2)}) collective-permute-start(bf16[32,512]{1,0:T(8,128)(2,1)S(1)} %bitcast.84), channel_id=1, source_target_pairs={{48,0},{0,16},{16,32},{32,48},{112,64},{64,80},{80,96},{96,112},{1... | collective-permute-start | bytes 98312 | tf_op jit(solution)/shard_map/ppermute | solution.py:27
  124.7 0.4 collective-permute-done.20
  125.1 3.1 %collective-permute-done.21 = bf16[32,512]{1,0:T(8,128)(2,1)S(1)} collective-permute-done((bf16[32,512]{1,0:T(8,128)(2,1)S(1)}, bf16[32,512]{1,0:T(8,128)(2,1)S(1)}, u32[]{:S(2)}, u32[]{:S(2)}) %collective-permute-start.21) | collective-permute-done | bytes 32800 | tf_op jit(solution)/shard_map/ppermute | solution.py:27
  128.3 4.5 %collective-permute-start.22 = (bf16[32,512]{1,0:T(8,128)(2,1)S(1)}, bf16[32,512]{1,0:T(8,128)(2,1)S(1)}, u32[]{:S(2)}, u32[]{:S(2)}) collective-permute-start(bf16[32,512]{1,0:T(8,128)(2,1)S(1)} %fusion.43), channel_id=1, source_target_pairs={{2,0},{3,1},{0,2},{1,3},{6,4},{7,5},{4,6},{5,7},{10,8},{11,9},{8,1... | collective-permute-start | bytes 98312 | tf_op jit(solution)/shard_map/ppermute | solution.py:41
  132.8 3.4 %collective-permute-done.22 = bf16[32,512]{1,0:T(8,128)(2,1)S(1)} collective-permute-done((bf16[32,512]{1,0:T(8,128)(2,1)S(1)}, bf16[32,512]{1,0:T(8,128)(2,1)S(1)}, u32[]{:S(2)}, u32[]{:S(2)}) %collective-permute-start.22) | collective-permute-done | bytes 32800 | tf_op jit(solution)/shard_map/ppermute | solution.py:41
  136.4 0.7 fusion.42
  137.1 2.3 %collective-permute-start.24 = (bf16[64,512]{1,0:T(8,128)(2,1)S(1)}, bf16[64,512]{1,0:T(8,128)(2,1)S(1)}, u32[]{:S(2)}, u32[]{:S(2)}) collective-permute-start(bf16[64,512]{1,0:T(8,128)(2,1)S(1)} %get-tuple-element.8), channel_id=1, source_target_pairs={{8,0},{9,1},{10,2},{11,3},{12,4},{13,5},{14,6},{15,7},{0,8},{1,9},... | collective-permute-start | bytes 196616 | tf_op jit(solution)/shard_map/ppermute | solution.py:41
  139.4 2.1 %collective-permute-start.25 = (bf16[64,512]{1,0:T(8,128)(2,1)S(1)}, bf16[64,512]{1,0:T(8,128)(2,1)S(1)}, u32[]{:S(2)}, u32[]{:S(2)}) collective-permute-start(bf16[64,512]{1,0:T(8,128)(2,1)S(1)} %get-tuple-element.8), channel_id=1, source_target_pairs={{12,0},{13,1},{14,2},{15,3},{0,4},{1,5},{2,6},{3,7},{4,8},{5,9},{6... | collective-permute-start | bytes 196616 | tf_op jit(solution)/shard_map/ppermute | solution.py:41
  141.5 0.4 collective-permute-done.23
  141.8 1.0 collective-permute-done.24
  142.9 1.0 constant_dynamic-update-slice_fusion.33
  143.9 4.1 %fusion.32 = bf16[512,512]{1,0:T(8,128)(2,1)S(1)} fusion(bf16[2048,512]{1,0:T(8,128)(2,1)} %constant_dynamic-update-slice_fusion.33, bf16[2048,2048]{1,0:T(8,128)(2,1)} %get-tuple-element.6), kind=kOutput, calls=%fused_computation.19 | convolution fusion | flops 1074003968 | bytes 4718592 | tf_op jit(solution)/shard_map/dot_general | solution.py:98
  148.0 3.6 %fusion.29 = bf16[512,512]{1,0:T(8,128)(2,1)S(1)} fusion(bf16[2048,512]{1,0:T(8,128)(2,1)} %constant_dynamic-update-slice_fusion.33, bf16[2048,2048]{1,0:T(8,128)(2,1)} %get-tuple-element.6), kind=kOutput, calls=%fused_computation.18 | convolution fusion | flops 1074003968 | bytes 4718592 | tf_op jit(solution)/shard_map/dot_general | solution.py:98
  151.7 1.2 fusion.26
  153.1 1.9 %collective-permute-start.33 = (bf16[512,512]{1,0:T(8,128)(2,1)S(1)}, bf16[512,512]{1,0:T(8,128)(2,1)S(1)}, u32[]{:S(2)}, u32[]{:S(2)}) collective-permute-start(bf16[512,512]{1,0:T(8,128)(2,1)S(1)} %fusion.29), channel_id=1, source_target_pairs={{192,0},{208,16},{224,32},{240,48},{0,64},{16,80},{32,96},{48,112}... | collective-permute-start | bytes 1572872 | tf_op jit(solution)/shard_map/ppermute | solution.py:27
  155.3 11.8 %collective-permute-done.34 = bf16[512,512]{1,0:T(8,128)(2,1)S(1)} collective-permute-done((bf16[512,512]{1,0:T(8,128)(2,1)S(1)}, bf16[512,512]{1,0:T(8,128)(2,1)S(1)}, u32[]{:S(2)}, u32[]{:S(2)}) %collective-permute-start.34) | collective-permute-done | bytes 524320 | tf_op jit(solution)/shard_map/ppermute | solution.py:27
  167.1 6.9 %collective-permute-done.33 = bf16[512,512]{1,0:T(8,128)(2,1)S(1)} collective-permute-done((bf16[512,512]{1,0:T(8,128)(2,1)S(1)}, bf16[512,512]{1,0:T(8,128)(2,1)S(1)}, u32[]{:S(2)}, u32[]{:S(2)}) %collective-permute-start.33) | collective-permute-done | bytes 524320 | tf_op jit(solution)/shard_map/ppermute | solution.py:27
  174.1 1.3 fusion.63
  175.4 2.0 %collective-permute-start.37 = (bf16[128,512]{1,0:T(8,128)(2,1)S(1)}, bf16[128,512]{1,0:T(8,128)(2,1)S(1)}, u32[]{:S(2)}, u32[]{:S(2)}) collective-permute-start(bf16[128,512]{1,0:T(8,128)(2,1)S(1)} %get-tuple-element.17), channel_id=1, source_target_pairs={{16,0},{32,16},{48,32},{0,48},{80,64},{96,80},{112,96},{64,112},{1... | collective-permute-start | bytes 393224 | tf_op jit(solution)/shard_map/ppermute | solution.py:27
  177.4 0.7 collective-permute-start.36
  178.1 0.8 collective-permute-start.35
  178.9 1.2 fusion.35
  180.1 0.4 collective-permute-done.37
  180.5 5.2 %collective-permute-done.36 = bf16[128,512]{1,0:T(8,128)(2,1)S(1)} collective-permute-done((bf16[128,512]{1,0:T(8,128)(2,1)S(1)}, bf16[128,512]{1,0:T(8,128)(2,1)S(1)}, u32[]{:S(2)}, u32[]{:S(2)}) %collective-permute-start.36) | collective-permute-done | bytes 131104 | tf_op jit(solution)/shard_map/ppermute | solution.py:27
  185.7 0.7 fusion.41
  (88 shorter events, 1.9 us)
Async XLA Ops:
  0.6 85.8 %copy-start = (bf16[512,512]{1,0:T(8,128)(2,1)S(1)}, bf16[512,512]{1,0:T(8,128)(2,1)}, u32[]{:S(2)}) copy-start(bf16[512,512]{1,0:T(8,128)(2,1)} %param.10) | copy-start | bytes 1572868
  0.6 8.9 %collective-permute-start = (bf16[128,512]{1,0:T(8,128)(2,1)}, bf16[128,512]{1,0:T(8,128)(2,1)S(1)}, u32[]{:S(2)}, u32[]{:S(2)}) collective-permute-start(bf16[128,512]{1,0:T(8,128)(2,1)} %bitcast.78), channel_id=1, source_target_pairs={{16,0},{32,16},{48,32},{0,48},{80,64},{96,80},{112,96},{64,112},{1... | collective-permute-start | bytes 393224 | tf_op jit(solution)/shard_map/ppermute | solution.py:27
  5.3 11.4 %collective-permute-start.1 = (bf16[128,512]{1,0:T(8,128)(2,1)}, bf16[128,512]{1,0:T(8,128)(2,1)S(1)}, u32[]{:S(2)}, u32[]{:S(2)}) collective-permute-start(bf16[128,512]{1,0:T(8,128)(2,1)} %bitcast.79), channel_id=1, source_target_pairs={{32,0},{48,16},{0,32},{16,48},{96,64},{112,80},{64,96},{80,112},{1... | collective-permute-start | bytes 393224 | tf_op jit(solution)/shard_map/ppermute | solution.py:27
  5.3 11.4 %collective-permute-start.2 = (bf16[128,512]{1,0:T(8,128)(2,1)}, bf16[128,512]{1,0:T(8,128)(2,1)S(1)}, u32[]{:S(2)}, u32[]{:S(2)}) collective-permute-start(bf16[128,512]{1,0:T(8,128)(2,1)} %bitcast.80), channel_id=1, source_target_pairs={{48,0},{0,16},{16,32},{32,48},{112,64},{64,80},{80,96},{96,112},{1... | collective-permute-start | bytes 393224 | tf_op jit(solution)/shard_map/ppermute | solution.py:27
  17.7 25.0 %collective-permute-start.3 = (bf16[512,512]{1,0:T(8,128)(2,1)S(1)}, bf16[512,512]{1,0:T(8,128)(2,1)S(1)}, u32[]{:S(2)}, u32[]{:S(2)}) collective-permute-start(bf16[512,512]{1,0:T(8,128)(2,1)S(1)} %pad_maximum_fusion), channel_id=1, source_target_pairs={{64,0},{80,16},{96,32},{112,48},{128,64},{144,80},{160,96},{176,11... | collective-permute-start | bytes 1572872 | tf_op jit(solution)/shard_map/ppermute | solution.py:27
  21.6 21.2 %collective-permute-start.4 = (bf16[512,512]{1,0:T(8,128)(2,1)S(1)}, bf16[512,512]{1,0:T(8,128)(2,1)S(1)}, u32[]{:S(2)}, u32[]{:S(2)}) collective-permute-start(bf16[512,512]{1,0:T(8,128)(2,1)S(1)} %pad_maximum_fusion), channel_id=1, source_target_pairs={{128,0},{144,16},{160,32},{176,48},{192,64},{208,80},{224,96},{240... | collective-permute-start | bytes 1572872 | tf_op jit(solution)/shard_map/ppermute | solution.py:27
  23.0 2.2 %copy-start.1 = (bf16[1,1,128,128,128]{4,3,2,1,0:T(8,128)(2,1)S(1)}, bf16[1,1,128,128,128]{4,3,2,1,0:T(8,128)(2,1)}, u32[]{:S(2)}) copy-start(bf16[1,1,128,128,128]{4,3,2,1,0:T(8,128)(2,1)} %param.9) | copy-start | bytes 12582916
  37.4 11.0 %collective-permute-start.5 = (bf16[512,512]{1,0:T(8,128)(2,1)S(1)}, bf16[512,512]{1,0:T(8,128)(2,1)S(1)}, u32[]{:S(2)}, u32[]{:S(2)}) collective-permute-start(bf16[512,512]{1,0:T(8,128)(2,1)S(1)} %pad_maximum_fusion), channel_id=1, source_target_pairs={{192,0},{208,16},{224,32},{240,48},{0,64},{16,80},{32,96},{48,112}... | collective-permute-start | bytes 1572872 | tf_op jit(solution)/shard_map/ppermute | solution.py:27
  50.8 2.7 %collective-permute-start.6 = (bf16[1024,512]{1,0:T(8,128)(2,1)S(1)}, bf16[1024,512]{1,0:T(8,128)(2,1)S(1)}, u32[]{:S(2)}, u32[]{:S(2)}) collective-permute-start(bf16[1024,512]{1,0:T(8,128)(2,1)S(1)} %fusion.14), channel_id=1, source_target_pairs={{1,0},{0,1},{3,2},{2,3},{5,4},{4,5},{7,6},{6,7},{9,8},{8,9},{11,10... | collective-permute-start | bytes 3145736 | tf_op jit(solution)/shard_map/ppermute | solution.py:41
  55.8 30.8 %copy-start.2 = (bf16[1,128,512]{2,1,0:T(8,128)(2,1)S(1)}, bf16[1,128,512]{2,1,0:T(8,128)(2,1)}, u32[]{:S(2)}) copy-start(bf16[1,128,512]{2,1,0:T(8,128)(2,1)} %param.11) | copy-start | bytes 393220
  55.9 10.3 %collective-permute-start.9 = (bf16[256,512]{1,0:T(8,128)(2,1)S(1)}, bf16[256,512]{1,0:T(8,128)(2,1)S(1)}, u32[]{:S(2)}, u32[]{:S(2)}) collective-permute-start(bf16[256,512]{1,0:T(8,128)(2,1)S(1)} %get-tuple-element.14), channel_id=1, source_target_pairs={{4,0},{5,1},{6,2},{7,3},{8,4},{9,5},{10,6},{11,7},{12,8},{13,9},{1... | collective-permute-start | bytes 786440 | tf_op jit(solution)/shard_map/ppermute | solution.py:41
  59.6 13.2 %collective-permute-start.8 = (bf16[256,512]{1,0:T(8,128)(2,1)S(1)}, bf16[256,512]{1,0:T(8,128)(2,1)S(1)}, u32[]{:S(2)}, u32[]{:S(2)}) collective-permute-start(bf16[256,512]{1,0:T(8,128)(2,1)S(1)} %get-tuple-element.15), channel_id=1, source_target_pairs={{8,0},{9,1},{10,2},{11,3},{12,4},{13,5},{14,6},{15,7},{0,8},{1,9},... | collective-permute-start | bytes 786440 | tf_op jit(solution)/shard_map/ppermute | solution.py:41
  60.8 12.0 %collective-permute-start.7 = (bf16[256,512]{1,0:T(8,128)(2,1)S(1)}, bf16[256,512]{1,0:T(8,128)(2,1)S(1)}, u32[]{:S(2)}, u32[]{:S(2)}) collective-permute-start(bf16[256,512]{1,0:T(8,128)(2,1)S(1)} %get-tuple-element.13), channel_id=1, source_target_pairs={{12,0},{13,1},{14,2},{15,3},{0,4},{1,5},{2,6},{3,7},{4,8},{5,9},{6... | collective-permute-start | bytes 786440 | tf_op jit(solution)/shard_map/ppermute | solution.py:41
  72.9 13.5 %collective-permute-start.10 = (bf16[128,512]{1,0:T(8,128)(2,1)S(1)}, bf16[128,512]{1,0:T(8,128)(2,1)S(1)}, u32[]{:S(2)}, u32[]{:S(2)}) collective-permute-start(bf16[128,512]{1,0:T(8,128)(2,1)S(1)} %slice.164), channel_id=1, source_target_pairs={{2,0},{3,1},{0,2},{1,3},{6,4},{7,5},{4,6},{5,7},{10,8},{11,9},{8,1... | collective-permute-start | bytes 393224 | tf_op jit(solution)/shard_map/ppermute | solution.py:41
  87.1 1.8 collective-permute-start.11
  89.0 10.5 %collective-permute-start.14 = (bf16[64,512]{1,0:T(8,128)(2,1)S(1)}, bf16[64,512]{1,0:T(8,128)(2,1)S(1)}, u32[]{:S(2)}, u32[]{:S(2)}) collective-permute-start(bf16[64,512]{1,0:T(8,128)(2,1)S(1)} %get-tuple-element.20), channel_id=1, source_target_pairs={{4,0},{5,1},{6,2},{7,3},{8,4},{9,5},{10,6},{11,7},{12,8},{13,9},{1... | collective-permute-start | bytes 196616 | tf_op jit(solution)/shard_map/ppermute | solution.py:41
  89.1 10.5 %collective-permute-start.13 = (bf16[64,512]{1,0:T(8,128)(2,1)S(1)}, bf16[64,512]{1,0:T(8,128)(2,1)S(1)}, u32[]{:S(2)}, u32[]{:S(2)}) collective-permute-start(bf16[64,512]{1,0:T(8,128)(2,1)S(1)} %get-tuple-element.21), channel_id=1, source_target_pairs={{8,0},{9,1},{10,2},{11,3},{12,4},{13,5},{14,6},{15,7},{0,8},{1,9},... | collective-permute-start | bytes 196616 | tf_op jit(solution)/shard_map/ppermute | solution.py:41
  93.9 5.7 %collective-permute-start.12 = (bf16[64,512]{1,0:T(8,128)(2,1)S(1)}, bf16[64,512]{1,0:T(8,128)(2,1)S(1)}, u32[]{:S(2)}, u32[]{:S(2)}) collective-permute-start(bf16[64,512]{1,0:T(8,128)(2,1)S(1)} %get-tuple-element.19), channel_id=1, source_target_pairs={{12,0},{13,1},{14,2},{15,3},{0,4},{1,5},{2,6},{3,7},{4,8},{5,9},{6... | collective-permute-start | bytes 196616 | tf_op jit(solution)/shard_map/ppermute | solution.py:41
  94.2 10.5 %collective-permute-start.27 = (bf16[128,512]{1,0:T(8,128)(2,1)S(1)}, bf16[128,512]{1,0:T(8,128)(2,1)S(1)}, u32[]{:S(2)}, u32[]{:S(2)}) collective-permute-start(bf16[128,512]{1,0:T(8,128)(2,1)S(1)} %get-tuple-element.34), channel_id=1, source_target_pairs={{2,0},{3,1},{0,2},{1,3},{6,4},{7,5},{4,6},{5,7},{10,8},{11,9},{8,1... | collective-permute-start | bytes 393224 | tf_op jit(solution)/shard_map/ppermute | solution.py:41
  99.6 11.3 %collective-permute-start.15 = (bf16[32,512]{1,0:T(8,128)(2,1)S(1)}, bf16[32,512]{1,0:T(8,128)(2,1)S(1)}, u32[]{:S(2)}, u32[]{:S(2)}) collective-permute-start(bf16[32,512]{1,0:T(8,128)(2,1)S(1)} %dynamic-slice_convert_fusion.4), channel_id=1, source_target_pairs={{2,0},{3,1},{0,2},{1,3},{6,4},{7,5},{4,6},{5,7},{10,8},{11,9},{8,1... | collective-permute-start | bytes 98312 | tf_op jit(solution)/shard_map/ppermute | solution.py:41
  104.7 17.8 %collective-permute-start.28 = (bf16[256,512]{1,0:T(8,128)(2,1)S(1)}, bf16[256,512]{1,0:T(8,128)(2,1)S(1)}, u32[]{:S(2)}, u32[]{:S(2)}) collective-permute-start(bf16[256,512]{1,0:T(8,128)(2,1)S(1)} %pad_maximum_fusion.1), channel_id=1, source_target_pairs={{4,0},{5,1},{6,2},{7,3},{8,4},{9,5},{10,6},{11,7},{12,8},{13,9},{1... | collective-permute-start | bytes 786440 | tf_op jit(solution)/shard_map/ppermute | solution.py:41
  108.2 16.3 %collective-permute-start.29 = (bf16[256,512]{1,0:T(8,128)(2,1)S(1)}, bf16[256,512]{1,0:T(8,128)(2,1)S(1)}, u32[]{:S(2)}, u32[]{:S(2)}) collective-permute-start(bf16[256,512]{1,0:T(8,128)(2,1)S(1)} %pad_maximum_fusion.1), channel_id=1, source_target_pairs={{8,0},{9,1},{10,2},{11,3},{12,4},{13,5},{14,6},{15,7},{0,8},{1,9},... | collective-permute-start | bytes 786440 | tf_op jit(solution)/shard_map/ppermute | solution.py:41
  108.2 16.4 %collective-permute-start.30 = (bf16[256,512]{1,0:T(8,128)(2,1)S(1)}, bf16[256,512]{1,0:T(8,128)(2,1)S(1)}, u32[]{:S(2)}, u32[]{:S(2)}) collective-permute-start(bf16[256,512]{1,0:T(8,128)(2,1)S(1)} %pad_maximum_fusion.1), channel_id=1, source_target_pairs={{12,0},{13,1},{14,2},{15,3},{0,4},{1,5},{2,6},{3,7},{4,8},{5,9},{6... | collective-permute-start | bytes 786440 | tf_op jit(solution)/shard_map/ppermute | solution.py:41
  110.9 4.0 %collective-permute-start.16 = (bf16[32,512]{1,0:T(8,128)(2,1)S(1)}, bf16[32,512]{1,0:T(8,128)(2,1)S(1)}, u32[]{:S(2)}, u32[]{:S(2)}) collective-permute-start(bf16[32,512]{1,0:T(8,128)(2,1)S(1)} %get-tuple-element.12), channel_id=1, source_target_pairs={{64,0},{80,16},{96,32},{112,48},{128,64},{144,80},{160,96},{176,11... | collective-permute-start | bytes 98312 | tf_op jit(solution)/shard_map/ppermute | solution.py:27
  111.1 5.5 %collective-permute-start.17 = (bf16[32,512]{1,0:T(8,128)(2,1)S(1)}, bf16[32,512]{1,0:T(8,128)(2,1)S(1)}, u32[]{:S(2)}, u32[]{:S(2)}) collective-permute-start(bf16[32,512]{1,0:T(8,128)(2,1)S(1)} %get-tuple-element.12), channel_id=1, source_target_pairs={{128,0},{144,16},{160,32},{176,48},{192,64},{208,80},{224,96},{240... | collective-permute-start | bytes 98312 | tf_op jit(solution)/shard_map/ppermute | solution.py:27
  114.9 5.1 %collective-permute-start.18 = (bf16[32,512]{1,0:T(8,128)(2,1)S(1)}, bf16[32,512]{1,0:T(8,128)(2,1)S(1)}, u32[]{:S(2)}, u32[]{:S(2)}) collective-permute-start(bf16[32,512]{1,0:T(8,128)(2,1)S(1)} %get-tuple-element.12), channel_id=1, source_target_pairs={{192,0},{208,16},{224,32},{240,48},{0,64},{16,80},{32,96},{48,112}... | collective-permute-start | bytes 98312 | tf_op jit(solution)/shard_map/ppermute | solution.py:27
  120.1 4.6 %collective-permute-start.19 = (bf16[32,512]{1,0:T(8,128)(2,1)S(1)}, bf16[32,512]{1,0:T(8,128)(2,1)S(1)}, u32[]{:S(2)}, u32[]{:S(2)}) collective-permute-start(bf16[32,512]{1,0:T(8,128)(2,1)S(1)} %bitcast.82), channel_id=1, source_target_pairs={{16,0},{32,16},{48,32},{0,48},{80,64},{96,80},{112,96},{64,112},{1... | collective-permute-start | bytes 98312 | tf_op jit(solution)/shard_map/ppermute | solution.py:27
  120.2 4.9 %collective-permute-start.20 = (bf16[32,512]{1,0:T(8,128)(2,1)S(1)}, bf16[32,512]{1,0:T(8,128)(2,1)S(1)}, u32[]{:S(2)}, u32[]{:S(2)}) collective-permute-start(bf16[32,512]{1,0:T(8,128)(2,1)S(1)} %bitcast.83), channel_id=1, source_target_pairs={{32,0},{48,16},{0,32},{16,48},{96,64},{112,80},{64,96},{80,112},{1... | collective-permute-start | bytes 98312 | tf_op jit(solution)/shard_map/ppermute | solution.py:27
  122.5 5.7 %collective-permute-start.21 = (bf16[32,512]{1,0:T(8,128)(2,1)S(1)}, bf16[32,512]{1,0:T(8,128)(2,1)S(1)}, u32[]{:S(2)}, u32[]{:S(2)}) collective-permute-start(bf16[32,512]{1,0:T(8,128)(2,1)S(1)} %bitcast.84), channel_id=1, source_target_pairs={{48,0},{0,16},{16,32},{32,48},{112,64},{64,80},{80,96},{96,112},{1... | collective-permute-start | bytes 98312 | tf_op jit(solution)/shard_map/ppermute | solution.py:27
  124.6 3.7 %copy-start.3 = (bf16[2048,512]{1,0:T(8,128)(2,1)}, bf16[2048,512]{1,0:T(8,128)(2,1)S(1)}, u32[]{:S(2)}) copy-start(bf16[2048,512]{1,0:T(8,128)(2,1)S(1)} %get-tuple-element.23) | copy-start | bytes 6291460
  124.6 18.3 %collective-permute-start.31 = (bf16[1024,512]{1,0:T(8,128)(2,1)S(1)}, bf16[1024,512]{1,0:T(8,128)(2,1)S(1)}, u32[]{:S(2)}, u32[]{:S(2)}) collective-permute-start(bf16[1024,512]{1,0:T(8,128)(2,1)S(1)} %get-tuple-element.22), channel_id=1, source_target_pairs={{1,0},{0,1},{3,2},{2,3},{5,4},{4,5},{7,6},{6,7},{9,8},{8,9},{11,10... | collective-permute-start | bytes 3145736 | tf_op jit(solution)/shard_map/ppermute | solution.py:41
  128.3 8.0 %collective-permute-start.22 = (bf16[32,512]{1,0:T(8,128)(2,1)S(1)}, bf16[32,512]{1,0:T(8,128)(2,1)S(1)}, u32[]{:S(2)}, u32[]{:S(2)}) collective-permute-start(bf16[32,512]{1,0:T(8,128)(2,1)S(1)} %fusion.43), channel_id=1, source_target_pairs={{2,0},{3,1},{0,2},{1,3},{6,4},{7,5},{4,6},{5,7},{10,8},{11,9},{8,1... | collective-permute-start | bytes 98312 | tf_op jit(solution)/shard_map/ppermute | solution.py:41
  136.3 5.6 %collective-permute-start.23 = (bf16[64,512]{1,0:T(8,128)(2,1)S(1)}, bf16[64,512]{1,0:T(8,128)(2,1)S(1)}, u32[]{:S(2)}, u32[]{:S(2)}) collective-permute-start(bf16[64,512]{1,0:T(8,128)(2,1)S(1)} %get-tuple-element.8), channel_id=1, source_target_pairs={{4,0},{5,1},{6,2},{7,3},{8,4},{9,5},{10,6},{11,7},{12,8},{13,9},{1... | collective-permute-start | bytes 196616 | tf_op jit(solution)/shard_map/ppermute | solution.py:41
  137.1 5.8 %collective-permute-start.24 = (bf16[64,512]{1,0:T(8,128)(2,1)S(1)}, bf16[64,512]{1,0:T(8,128)(2,1)S(1)}, u32[]{:S(2)}, u32[]{:S(2)}) collective-permute-start(bf16[64,512]{1,0:T(8,128)(2,1)S(1)} %get-tuple-element.8), channel_id=1, source_target_pairs={{8,0},{9,1},{10,2},{11,3},{12,4},{13,5},{14,6},{15,7},{0,8},{1,9},... | collective-permute-start | bytes 196616 | tf_op jit(solution)/shard_map/ppermute | solution.py:41
  139.4 15.7 %collective-permute-start.25 = (bf16[64,512]{1,0:T(8,128)(2,1)S(1)}, bf16[64,512]{1,0:T(8,128)(2,1)S(1)}, u32[]{:S(2)}, u32[]{:S(2)}) collective-permute-start(bf16[64,512]{1,0:T(8,128)(2,1)S(1)} %get-tuple-element.8), channel_id=1, source_target_pairs={{12,0},{13,1},{14,2},{15,3},{0,4},{1,5},{2,6},{3,7},{4,8},{5,9},{6... | collective-permute-start | bytes 196616 | tf_op jit(solution)/shard_map/ppermute | solution.py:41
  142.9 8.7 %slice-start = ((s8[8388608]{0:T(1024)(128)(4,1)}), s8[4194304]{0:T(1024)(128)(4,1)S(1)}, s32[]{:S(2)}) async-start(s8[8388608]{0:T(1024)(128)(4,1)} %bitcast.85), calls=%async_computation | async-start | bytes 8388608
  143.9 7.7 %slice-start.1 = ((s8[8388608]{0:T(1024)(128)(4,1)}), s8[4194304]{0:T(1024)(128)(4,1)S(1)}, s32[]{:S(2)}) async-start(s8[8388608]{0:T(1024)(128)(4,1)} %bitcast.85), calls=%async_computation.1 | async-start | bytes 8388608
  148.0 3.7 %copy-start.4 = (bf16[2048,512]{1,0:T(8,128)(2,1)S(1)}, bf16[2048,512]{1,0:T(8,128)(2,1)}, u32[]{:S(2)}) copy-start(bf16[2048,512]{1,0:T(8,128)(2,1)} %constant_dynamic-update-slice_fusion.33) | copy-start | bytes 6291460
  152.9 14.2 %collective-permute-start.34 = (bf16[512,512]{1,0:T(8,128)(2,1)S(1)}, bf16[512,512]{1,0:T(8,128)(2,1)S(1)}, u32[]{:S(2)}, u32[]{:S(2)}) collective-permute-start(bf16[512,512]{1,0:T(8,128)(2,1)S(1)} %fusion.32), channel_id=1, source_target_pairs={{64,0},{80,16},{96,32},{112,48},{128,64},{144,80},{160,96},{176,11... | collective-permute-start | bytes 1572872 | tf_op jit(solution)/shard_map/ppermute | solution.py:27
  153.1 20.9 %collective-permute-start.33 = (bf16[512,512]{1,0:T(8,128)(2,1)S(1)}, bf16[512,512]{1,0:T(8,128)(2,1)S(1)}, u32[]{:S(2)}, u32[]{:S(2)}) collective-permute-start(bf16[512,512]{1,0:T(8,128)(2,1)S(1)} %fusion.29), channel_id=1, source_target_pairs={{192,0},{208,16},{224,32},{240,48},{0,64},{16,80},{32,96},{48,112}... | collective-permute-start | bytes 1572872 | tf_op jit(solution)/shard_map/ppermute | solution.py:27
  155.0 19.0 %collective-permute-start.32 = (bf16[512,512]{1,0:T(8,128)(2,1)S(1)}, bf16[512,512]{1,0:T(8,128)(2,1)S(1)}, u32[]{:S(2)}, u32[]{:S(2)}) collective-permute-start(bf16[512,512]{1,0:T(8,128)(2,1)S(1)} %fusion.26), channel_id=1, source_target_pairs={{128,0},{144,16},{160,32},{176,48},{192,64},{208,80},{224,96},{240... | collective-permute-start | bytes 1572872 | tf_op jit(solution)/shard_map/ppermute | solution.py:27
  155.2 23.7 %collective-permute-start.26 = (bf16[256,512]{1,0:T(8,128)(2,1)S(1)}, bf16[256,512]{1,0:T(8,128)(2,1)S(1)}, u32[]{:S(2)}, u32[]{:S(2)}) collective-permute-start(bf16[256,512]{1,0:T(8,128)(2,1)S(1)} %constant_dynamic-slice_fusion), channel_id=1, source_target_pairs={{1,0},{0,1},{3,2},{2,3},{5,4},{4,5},{7,6},{6,7},{9,8},{8,9},{11,10... | collective-permute-start | bytes 786440 | tf_op jit(solution)/shard_map/ppermute | solution.py:41
  175.4 5.0 %collective-permute-start.37 = (bf16[128,512]{1,0:T(8,128)(2,1)S(1)}, bf16[128,512]{1,0:T(8,128)(2,1)S(1)}, u32[]{:S(2)}, u32[]{:S(2)}) collective-permute-start(bf16[128,512]{1,0:T(8,128)(2,1)S(1)} %get-tuple-element.17), channel_id=1, source_target_pairs={{16,0},{32,16},{48,32},{0,48},{80,64},{96,80},{112,96},{64,112},{1... | collective-permute-start | bytes 393224 | tf_op jit(solution)/shard_map/ppermute | solution.py:27
  177.4 8.2 %collective-permute-start.36 = (bf16[128,512]{1,0:T(8,128)(2,1)S(1)}, bf16[128,512]{1,0:T(8,128)(2,1)S(1)}, u32[]{:S(2)}, u32[]{:S(2)}) collective-permute-start(bf16[128,512]{1,0:T(8,128)(2,1)S(1)} %get-tuple-element.18), channel_id=1, source_target_pairs={{32,0},{48,16},{0,32},{16,48},{96,64},{112,80},{64,96},{80,112},{1... | collective-permute-start | bytes 393224 | tf_op jit(solution)/shard_map/ppermute | solution.py:27
  178.1 7.6 %collective-permute-start.35 = (bf16[128,512]{1,0:T(8,128)(2,1)S(1)}, bf16[128,512]{1,0:T(8,128)(2,1)S(1)}, u32[]{:S(2)}, u32[]{:S(2)}) collective-permute-start(bf16[128,512]{1,0:T(8,128)(2,1)S(1)} %get-tuple-element.16), channel_id=1, source_target_pairs={{48,0},{0,16},{16,32},{32,48},{112,64},{64,80},{80,96},{96,112},{1... | collective-permute-start | bytes 393224 | tf_op jit(solution)/shard_map/ppermute | solution.py:27
